TPU v7x, 512 devices: a whole 4x4x16 slice. The times are simulated.
512 devices in a mesh: pipe: 4 (over z_hi), dp: 16 (over y, x), tensor: 8 (over z_lo, core).
Axes of the slice: x: 4, y: 4, z: 16 (z_hi: 4, z_lo: 4; z = z_hi * 4 + z_lo), core: 2. Of those that a mesh axis runs over, the one named last changes fastest.
Arguments:
- x_in: bfloat16 [4, 2, 16, 128, 1600], P('pipe', None, 'dp', 'tensor'), may hold values from -6 to 6
- out_grad: bfloat16 [2, 16, 128, 1600], P(None, 'dp'), may hold values from -6 to 6
- layer_scale: float32 [4, 1600], P('pipe'), may hold values from 0.05 to 1
- norm_gain: float32 [4, 1600], P('pipe'), may hold values from 0.5 to 1.5
- master: float32 [4, 1600, 8192], P('pipe', 'dp', 'tensor'), may hold values from -0.15625 to 0.15625
- moment_one: float32 [4, 1600, 8192], P('pipe', 'dp', 'tensor'), may hold values from -4 to 4
- moment_two: float32 [4, 1600, 8192], P('pipe', 'dp', 'tensor'), may hold values from 0.05 to 5
Outputs:
- input_grads: bfloat16 [4, 2, 16, 128, 1600], P('pipe', None, 'dp', 'tensor')
- new_master: float32 [4, 1600, 8192], P('pipe', 'dp', 'tensor')
- new_moment_one: float32 [4, 1600, 8192], P('pipe', 'dp', 'tensor')
- new_moment_two: float32 [4, 1600, 8192], P('pipe', 'dp', 'tensor')
- scale_grads: float32 [4, 2, 1600], P('pipe')
All inputs are finite; a program needn't handle non-finite values.
Results may differ from a plain program's by a relative error of at most 0.027.
Values may be sent and summed in bfloat16 or wider, within the bound.
A program may use at most 128 MiB of HBM per device.

v0:
```python
import math
import jax
import jax.numpy as jnp
from jax import lax
from jax.sharding import PartitionSpec as P

HD = 128
beta_one = 0.9
beta_two = 0.95
adam_eps = 1e-08
learn_rate = 0.001
weight_decay = 0.05
adam_step = 100.0
norm_eps = 1e-06


def from_behind(block, axis, distance):
    devices = range(lax.axis_size(axis))
    route = [(i - distance, i) for i in devices if i - distance in devices]
    return lax.ppermute(block, axis, route)


def normalize(values_in):
    inverse = lax.rsqrt(jnp.mean(values_in * values_in, axis=-1, keepdims=True) + norm_eps)
    return (inverse, values_in * inverse)


def select_micro(array, micro_index):
    return lax.dynamic_index_in_dim(array, micro_index, 0, keepdims=False)


def store_slot(buffer, value, slot_index):
    return lax.dynamic_update_index_in_dim(buffer, value, slot_index, 0)


def local(x_in, out_grad, layer_scale, norm_gain, master, moment_one, moment_two):
    n_pipe = lax.axis_size("pipe")
    n_tensor = lax.axis_size("tensor")
    pipe_rank = lax.axis_index("pipe")
    micro_count = x_in.shape[1]
    images = x_in.shape[2]
    shard_len = x_in.shape[3]
    channels = x_in.shape[4]
    seq_len = shard_len * n_tensor
    row_start = lax.axis_index("tensor") * shard_len
    head_cols = master.shape[2] // 4
    local_heads = head_cols // HD
    score_root = math.sqrt(HD)
    scale_vec = layer_scale[0]
    gain_vec = norm_gain[0]
    weights = lax.all_gather(master[0].astype(jnp.bfloat16), "dp", axis=0, tiled=True)
    w_qkv = weights[:, : 3 * head_cols]
    w_out = weights[:, 3 * head_cols :]
    full_x = lax.all_gather(x_in[0], "tensor", axis=2, tiled=True).astype(jnp.float32)
    full_inverse, full_unit = normalize(full_x)
    normed = (full_unit * gain_vec).astype(jnp.bfloat16)
    local_unit = lax.dynamic_slice_in_dim(full_unit, row_start, shard_len, 2)
    projected = jnp.einsum(
        "mbsd,dc->mbsc", normed, w_qkv, preferred_element_type=jnp.float32
    ).astype(jnp.bfloat16)
    projected = projected.reshape(micro_count, images, seq_len, 3, local_heads, HD)
    query = projected[:, :, :, 0]
    keys = projected[:, :, :, 1]
    values = projected[:, :, :, 2]
    scores = (
        jnp.einsum("mbqhe,mbkhe->mbhqk", query, keys, preferred_element_type=jnp.float32)
        / score_root
    )
    probs = jax.nn.softmax(scores, axis=-1)
    probs_low = probs.astype(jnp.bfloat16)
    attended = jnp.einsum(
        "mbhqk,mbkhe->mbqhe", probs_low, values, preferred_element_type=jnp.float32
    ).astype(jnp.bfloat16)
    attended_flat = attended.reshape(micro_count, images, seq_len, head_cols)

    def backward_segment(micro_index, incoming):
        query_now = select_micro(query, micro_index)
        keys_now = select_micro(keys, micro_index)
        values_now = select_micro(values, micro_index)
        probs_now = select_micro(probs, micro_index)
        probs_low_now = select_micro(probs_low, micro_index)
        attended_now = select_micro(attended, micro_index)
        scaled = (scale_vec * incoming.astype(jnp.float32)).astype(jnp.bfloat16)
        d_att = jnp.einsum("bsd,dc->bsc", scaled, w_out, preferred_element_type=jnp.float32).astype(
            jnp.bfloat16
        )
        d_att = d_att.reshape(images, seq_len, local_heads, HD)
        d_prob = jnp.einsum(
            "bqhe,bkhe->bhqk", d_att, values_now, preferred_element_type=jnp.float32
        )
        row_delta = jnp.einsum(
            "bqhe,bqhe->bhq", d_att, attended_now, preferred_element_type=jnp.float32
        )
        d_score = (probs_now * (d_prob - row_delta[..., None]) / score_root).astype(jnp.bfloat16)
        d_query = jnp.einsum(
            "bhqk,bkhe->bqhe", d_score, keys_now, preferred_element_type=jnp.float32
        ).astype(jnp.bfloat16)
        d_keys = jnp.einsum(
            "bhqk,bqhe->bkhe", d_score, query_now, preferred_element_type=jnp.float32
        ).astype(jnp.bfloat16)
        d_values = jnp.einsum(
            "bhqk,bqhe->bkhe", probs_low_now, d_att, preferred_element_type=jnp.float32
        ).astype(jnp.bfloat16)
        d_proj = jnp.concatenate([d_query, d_keys, d_values], axis=2).reshape(
            images, seq_len, 3 * head_cols
        )
        partial_sum = jnp.einsum("bsc,dc->bsd", d_proj, w_qkv, preferred_element_type=jnp.float32)
        return (partial_sum, d_proj, scaled)

    def spare_segment(micro_index, incoming):
        return (
            jnp.zeros((images, seq_len, channels), jnp.float32),
            jnp.zeros((images, seq_len, 3 * head_cols), jnp.bfloat16),
            jnp.zeros((images, seq_len, channels), jnp.bfloat16),
        )

    segments = n_pipe + micro_count - 1
    is_last = pipe_rank == n_pipe - 1
    received = jnp.zeros((images, seq_len, channels), jnp.bfloat16)
    slots = micro_count + 1
    grads_out = jnp.zeros((slots, images, shard_len, channels), jnp.bfloat16)
    proj_saved = jnp.zeros((slots, images, seq_len, 3 * head_cols), jnp.bfloat16)
    scaled_saved = jnp.zeros((slots, images, seq_len, channels), jnp.bfloat16)
    grad_saved = jnp.zeros((slots, images, seq_len, channels), jnp.bfloat16)
    gain_part = jnp.zeros((channels,), jnp.float32)
    for segment_step in range(segments):
        micro_index = segment_step - (n_pipe - 1) + pipe_rank
        active = jnp.logical_and(micro_index >= 0, micro_index < micro_count)
        micro_index = jnp.clip(micro_index, 0, micro_count - 1)
        slot_index = jnp.where(active, micro_index, micro_count)
        arrived = received
        incoming = jnp.where(is_last, select_micro(out_grad, micro_index), arrived)
        partial_sum, d_proj, scaled = lax.cond(
            active, backward_segment, spare_segment, micro_index, incoming
        )
        pieces = partial_sum.astype(jnp.bfloat16).reshape(images, n_tensor, shard_len, channels)
        landed = lax.all_to_all(pieces, "tensor", split_axis=1, concat_axis=1, tiled=True)
        own_d = jnp.sum(landed.astype(jnp.float32), axis=1)
        d_normed = lax.all_gather(own_d.astype(jnp.bfloat16), "tensor", axis=1, tiled=True).astype(
            own_d.dtype
        )
        own_unit = select_micro(local_unit, micro_index)
        sel_unit = select_micro(full_unit, micro_index)
        sel_inverse = select_micro(full_inverse, micro_index)
        d_unit = d_normed * gain_vec
        d_input = sel_inverse * (
            d_unit - sel_unit * jnp.mean(d_unit * sel_unit, axis=-1, keepdims=True)
        )
        passed = (incoming.astype(jnp.float32) + d_input).astype(jnp.bfloat16)
        own_passed = lax.dynamic_slice_in_dim(passed, row_start, shard_len, 1)
        gain_part = gain_part + jnp.where(active, jnp.sum(own_d * own_unit, axis=(0, 1)), 0.0)
        grads_out = store_slot(grads_out, own_passed, slot_index)
        proj_saved = store_slot(proj_saved, d_proj, slot_index)
        scaled_saved = store_slot(scaled_saved, scaled, slot_index)
        grad_saved = store_slot(grad_saved, incoming, slot_index)
        if segment_step + 1 < segments:
            received = from_behind(passed, "pipe", -1)
    grads_kept = grads_out[:micro_count]
    proj_kept = proj_saved[:micro_count]
    scaled_kept = scaled_saved[:micro_count]
    grad_kept = grad_saved[:micro_count]
    grad_qkv = jnp.einsum("mbsd,mbsc->dc", normed, proj_kept, preferred_element_type=jnp.float32)
    grad_out = jnp.einsum(
        "mbsd,mbsc->dc", scaled_kept, attended_flat, preferred_element_type=jnp.float32
    )
    weight_grad = lax.psum_scatter(
        jnp.concatenate([grad_qkv, grad_out], axis=1).astype(jnp.bfloat16),
        "dp",
        scatter_dimension=0,
        tiled=True,
    ).astype(jnp.float32)
    summed_out = jnp.einsum(
        "mbsd,mbsc->dc", grad_kept, attended_flat, preferred_element_type=jnp.float32
    )
    scale_part = jnp.sum(w_out.astype(jnp.float32) * summed_out, axis=1)
    scale_grad, gain_grad = lax.psum((scale_part, gain_part), ("dp", "tensor"))
    bias_one = 1.0 - beta_one**adam_step
    bias_two = 1.0 - beta_two**adam_step
    first_new = beta_one * moment_one[0] + (1.0 - beta_one) * weight_grad
    second_new = beta_two * moment_two[0] + (1.0 - beta_two) * weight_grad * weight_grad
    update = first_new / bias_one / (jnp.sqrt(second_new / bias_two) + adam_eps)
    master_new = master[0] - learn_rate * (update + weight_decay * master[0])
    scale_both = jnp.stack([scale_grad, gain_grad])
    return (grads_kept[None], master_new[None], first_new[None], second_new[None], scale_both[None])


def solution(mesh):
    placed = (
        P("pipe", None, "dp", "tensor", None),
        P(None, "dp", None, None),
        P("pipe", None),
        P("pipe", None),
        P("pipe", "dp", "tensor"),
        P("pipe", "dp", "tensor"),
        P("pipe", "dp", "tensor"),
    )
    return jax.shard_map(
        local,
        mesh=mesh,
        in_specs=placed,
        out_specs=(
            P("pipe", None, "dp", "tensor", None),
            P("pipe", "dp", "tensor"),
            P("pipe", "dp", "tensor"),
            P("pipe", "dp", "tensor"),
            P("pipe", None, None),
        ),
        check_vma=False,
    )
```

profile of v0, /device:TPU:128, one launch (start us, length us, event | category | flops | bytes accessed | tf_op | source)
XLA Modules:
  0.0 1397.1 jit_solution(9497189529222593364)
XLA Ops:
  9.8 17.2 %all-gather = bf16[1,2,1,128,1600]{4,3,2,1,0:T(8,128)(2,1)S(1)} all-gather(bf16[1,2,1,16,1600]{4,3,2,1,0:T(8,128)(2,1)} %param.17), channel_id=2, replica_groups=mesh['pipe'=4,'dp'=16,'tensor'=8] {'tensor'}, dimensions={3}, use_global_device_ids=true | all-gather | bytes 921600 | tf_op jit(solution)/shard_map/all_gather | solution.py:54
  28.1 50.7 %all-gather.9.cloned.1.call-done = bf16[16,100,1024]{2,1,0:T(8,128)(2,1)} async-done(((bf16[1,100,1024]{2,1,0:T(8,128)(2,1)}), bf16[16,100,1024]{2,1,0:T(8,128)(2,1)}) %all-gather.9.cloned.1.call-update) | async-done | bytes 3276816 | tf_op jit(solution)/shard_map/all_gather | solution.py:51
  78.8 2.9 reshape.819
  81.7 3.4 fusion.113
  96.1 2.1 convolution_convert_fusion.20
  98.2 2.3 conditional.5
  100.5 2.0 copy.213
  102.5 4.8 all-to-all-start
  108.7 2.3 constant_dynamic-slice_fusion
  111.4 2.4 copy.217
  115.1 5.5 all-to-all-done
  122.4 15.6 %all-gather.1 = bf16[128,1600]{1,0:T(8,128)(2,1)} all-gather(bf16[16,1600]{1,0:T(8,128)(2,1)S(1)} %convert_element_type.421), channel_id=3, replica_groups=mesh['pipe'=4,'dp'=16,'tensor'=8] {'tensor'}, dimensions={0}, use_global_device_ids=true | all-gather | bytes 460800 | tf_op jit(solution)/shard_map/all_gather | solution.py:139
  138.0 1.9 copy.216
  141.5 2.2 fusion.145
  143.8 2.1 collective-permute-start
  147.2 39.6 %collective-permute-done = bf16[1,128,1600]{1,2,0:T(8,128)(2,1)} collective-permute-done((bf16[1,128,1600]{1,2,0:T(8,128)(2,1)}, bf16[1,128,1600]{1,2,0:T(8,128)(2,1)}, u32[]{:S(2)}, u32[]{:S(2)}) %collective-permute-start) | collective-permute-done | bytes 409632 | tf_op jit(solution)/shard_map/ppermute | solution.py:20
  186.9 1.9 bitcast_dynamic-update-slice_fusion.2
  189.9 2.7 conditional.6
  192.6 2.0 copy.227
  194.6 4.1 all-to-all-start.1
  198.7 2.4 copy.231
  201.1 10.9 all-to-all-done.1
  213.7 15.6 %all-gather.2 = bf16[128,1600]{1,0:T(8,128)(2,1)} all-gather(bf16[16,1600]{1,0:T(8,128)(2,1)S(1)} %convert_element_type.429), channel_id=4, replica_groups=mesh['pipe'=4,'dp'=16,'tensor'=8] {'tensor'}, dimensions={0}, use_global_device_ids=true | all-gather | bytes 460800 | tf_op jit(solution)/shard_map/all_gather | solution.py:139
  229.2 2.0 copy.230
  232.9 2.2 fusion.139
  235.1 2.2 collective-permute-start.1
  237.3 98.2 %collective-permute-done.1 = bf16[1,128,1600]{1,2,0:T(8,128)(2,1)} collective-permute-done((bf16[1,128,1600]{1,2,0:T(8,128)(2,1)}, bf16[1,128,1600]{1,2,0:T(8,128)(2,1)}, u32[]{:S(2)}, u32[]{:S(2)}) %collective-permute-start.1) | collective-permute-done | bytes 409632 | tf_op jit(solution)/shard_map/ppermute | solution.py:20
  335.5 2.1 bitcast_dynamic-update-slice_fusion.1
  337.7 34.1 %conditional.7 = (bf16[1,128,1600]{1,2,0:T(8,128)(2,1)}, bf16[1,1,128,768]{3,2,0,1:T(8,128)(2,1)}, bf16[1,1,128,1600]{2,3,0,1:T(8,128)(2,1)}) conditional(s32[]{:T(128)} %convert_element_type.434, () %tuple.72, (s32[]{:T(128)}, bf16[2,1,128,2,128]{4,2,3,0,1:T(8,128)(2,1)}, f32[2,1,2,128,128]{3,4,2,0,1:T(8,128)S(1)}, f32[1,1600]{1,0:T(1,128)S(1)}, ...), branch_computations={%region_11.12_spmd, %region_12.13_spmd} | conditional | flops 454803200 | bytes 11565162 | solution.py:133
  337.7 2.0 copy.236
  340.3 1.9 convolution_convert_fusion.8
  369.8 2.0 copy.364
  371.8 2.0 copy.241
  373.8 4.1 all-to-all-start.2
  377.9 2.3 copy.245
  380.3 2.3 copy.259
  382.6 2.4 copy.273
  399.1 16.0 %all-gather.3 = bf16[128,1600]{1,0:T(8,128)(2,1)} all-gather(bf16[16,1600]{1,0:T(8,128)(2,1)S(1)} %convert_element_type.437), channel_id=5, replica_groups=mesh['pipe'=4,'dp'=16,'tensor'=8] {'tensor'}, dimensions={0}, use_global_device_ids=true | all-gather | bytes 460800 | tf_op jit(solution)/shard_map/all_gather | solution.py:139
  415.0 1.9 copy.244
  425.6 38.5 %collective-permute-done.2 = bf16[1,128,1600]{1,2,0:T(8,128)(2,1)S(1)} collective-permute-done((bf16[1,128,1600]{1,2,0:T(8,128)(2,1)S(1)}, bf16[1,128,1600]{1,2,0:T(8,128)(2,1)S(1)}, u32[]{:S(2)}, u32[]{:S(2)}) %collective-permute-start.2) | collective-permute-done | bytes 409632 | tf_op jit(solution)/shard_map/ppermute | solution.py:20
  465.1 34.2 %conditional.8 = (bf16[1,128,1600]{1,2,0:T(8,128)(2,1)}, bf16[1,1,128,768]{3,2,0,1:T(8,128)(2,1)}, bf16[1,1,128,1600]{2,3,0,1:T(8,128)(2,1)}) conditional(s32[]{:T(128)} %convert_element_type.442, () %tuple.74, (s32[]{:T(128)}, bf16[2,1,128,2,128]{4,2,3,0,1:T(8,128)(2,1)}, f32[2,1,2,128,128]{3,4,2,0,1:T(8,128)S(1)}, f32[1,1600]{1,0:T(1,128)S(1)}, ...), branch_computations={%region_15.16_spmd, %region_16.17_spmd} | conditional | flops 454803200 | bytes 11565162 | solution.py:133
  465.2 2.0 copy.250
  467.8 1.9 convolution_convert_fusion.12
  497.4 1.9 copy.368
  499.3 2.0 copy.255
  501.3 4.1 all-to-all-start.3
  505.4 1.9 dynamic-slice_bitcast_fusion.2
  524.3 16.0 %all-gather.4 = bf16[128,1600]{1,0:T(8,128)(2,1)} all-gather(bf16[16,1600]{1,0:T(8,128)(2,1)S(1)} %convert_element_type.445), channel_id=6, replica_groups=mesh['pipe'=4,'dp'=16,'tensor'=8] {'tensor'}, dimensions={0}, use_global_device_ids=true | all-gather | bytes 460800 | tf_op jit(solution)/shard_map/all_gather | solution.py:139
  540.3 1.9 copy.258
  543.9 2.2 fusion.127
  546.1 2.1 collective-permute-start.3
  548.2 1.9 dynamic-slice_bitcast_fusion
  553.3 36.9 %collective-permute-done.3 = bf16[1,128,1600]{1,2,0:T(8,128)(2,1)} collective-permute-done((bf16[1,128,1600]{1,2,0:T(8,128)(2,1)}, bf16[1,128,1600]{1,2,0:T(8,128)(2,1)}, u32[]{:S(2)}, u32[]{:S(2)}) %collective-permute-start.3) | collective-permute-done | bytes 409632 | tf_op jit(solution)/shard_map/ppermute | solution.py:20
  590.2 2.2 bitcast_dynamic-update-slice_fusion.3
  592.4 2.3 conditional.9
  594.7 2.0 copy.269
  596.7 4.1 all-to-all-start.4
  602.5 1.9 bitcast_convert_fusion
  608.2 76.2 %fusion = bf16[112,1024]{1,0:T(8,128)(2,1)} fusion(bf16[1600,1024]{1,0:T(8,128)(2,1)S(1)} %pad_maximum_fusion.5), kind=kCustom, calls=%all-reduce-scatter | all-reduce-scatter fusion | flops 1835009 | bytes 3508224
  685.4 3.7 collective-permute-start.4
  689.1 4.1 collective-permute-start.5
  693.2 2.0 fusion.112
  703.2 15.6 %all-gather.5 = bf16[128,1600]{1,0:T(8,128)(2,1)S(1)} all-gather(bf16[16,1600]{1,0:T(8,128)(2,1)S(1)} %get-tuple-element.430), channel_id=7, replica_groups=mesh['pipe'=4,'dp'=16,'tensor'=8] {'tensor'}, dimensions={0}, use_global_device_ids=true | all-gather | bytes 460800 | tf_op jit(solution)/shard_map/all_gather | solution.py:139
  721.0 668.4 %all-reduce.2 = (f32[1,1600]{1,0:T(1,128)S(1)}, f32[1,1600]{1,0:T(1,128)S(1)}) all-reduce(f32[1,1600]{1,0:T(1,128)S(1)} %stack.10, f32[1,1600]{1,0:T(1,128)S(1)} %stack.9), channel_id=1, replica_groups=mesh['pipe'=4,'dp'=16,'tensor'=8] {'dp','tensor'}, use_global_device_ids=true, to_apply=%region_31.32 | all-reduce | flops 3200 | bytes 25600 | tf_op jit(solution)/shard_map/psum | solution.py:176
  (215 shorter events, 151.9 us)
Async XLA Ops:
  7.2 20.1 %copy-start.2 = (bf16[2,1,128,1600]{2,3,1,0:T(8,128)(2,1)S(1)}, bf16[2,1,128,1600]{2,3,1,0:T(8,128)(2,1)}, u32[]{:S(2)}) copy-start(bf16[2,1,128,1600]{2,3,1,0:T(8,128)(2,1)} %param.18) | copy-start | bytes 2457604
  7.2 71.6 %all-gather.9.cloned.1.call-start = ((), (), s32[]{:S(2)}) async-start(), calls=%async_computation.5 | async-start | bytes 3620864 | tf_op jit(solution)/shard_map/all_gather | solution.py:51
  27.0 1.1 copy-start.5
  27.3 54.4 %copy-start.44 = (f32[2,128]{1,0:T(2,128)}, f32[2,128]{1,0:T(2,128)S(1)}, u32[]{:S(2)}) copy-start(f32[2,128]{1,0:T(2,128)S(1)} %add_rsqrt_fusion) | copy-start | bytes 3076
  81.7 3.5 copy-start.1
  88.3 0.8 copy-start.35
  88.3 5.4 copy-start.34
  93.7 4.5 copy-start.42
  102.5 18.2 %all-to-all-start = ((bf16[1,8,16,1600]{3,2,0,1:T(8,128)(2,1)}), bf16[1,8,16,1600]{3,2,0,1:T(8,128)(2,1)}, u32[]{:S(2)}, u32[]{:S(2)}) async-start(bf16[1,8,16,1600]{3,2,0,1:T(8,128)(2,1)} %bitcast.535), calls=%async_computation | async-start | bytes 851968 | tf_op jit(solution)/shard_map/all_to_all | solution.py:137
  108.6 2.7 copy-start
  121.7 0.6 copy-start.26
  139.9 1.6 copy-start.11
  143.8 43.1 %collective-permute-start = (bf16[1,128,1600]{1,2,0:T(8,128)(2,1)}, bf16[1,128,1600]{1,2,0:T(8,128)(2,1)}, u32[]{:S(2)}, u32[]{:S(2)}) collective-permute-start(bf16[1,128,1600]{1,2,0:T(8,128)(2,1)} %fusion.145), channel_id=1, source_target_pairs={{128,0},{256,128},{384,256},{129,1},{257,129},{385,257},{130,2},{2... | collective-permute-start | bytes 1228808 | tf_op jit(solution)/shard_map/ppermute | solution.py:20
  145.9 41.0 %copy-start.3 = (bf16[2,1,128,1600]{2,3,1,0:T(8,128)(2,1)S(1)}, bf16[2,1,128,1600]{2,3,1,0:T(8,128)(2,1)}, u32[]{:S(2)}) copy-start(bf16[2,1,128,1600]{2,3,1,0:T(8,128)(2,1)} %param.18) | copy-start | bytes 2457604
  188.8 1.1 copy-start.25
  194.6 17.4 %all-to-all-start.1 = ((bf16[1,8,16,1600]{3,2,0,1:T(8,128)(2,1)}), bf16[1,8,16,1600]{3,2,0,1:T(8,128)(2,1)}, u32[]{:S(2)}, u32[]{:S(2)}) async-start(bf16[1,8,16,1600]{3,2,0,1:T(8,128)(2,1)} %bitcast.537), calls=%async_computation.1 | async-start | bytes 851968 | tf_op jit(solution)/shard_map/all_to_all | solution.py:137
  213.0 0.6 copy-start.28
  231.2 1.6 copy-start.9
  235.1 100.4 %collective-permute-start.1 = (bf16[1,128,1600]{1,2,0:T(8,128)(2,1)}, bf16[1,128,1600]{1,2,0:T(8,128)(2,1)}, u32[]{:S(2)}, u32[]{:S(2)}) collective-permute-start(bf16[1,128,1600]{1,2,0:T(8,128)(2,1)} %fusion.139), channel_id=1, source_target_pairs={{128,0},{256,128},{384,256},{129,1},{257,129},{385,257},{130,2},{2... | collective-permute-start | bytes 1228808 | tf_op jit(solution)/shard_map/ppermute | solution.py:20
  364.7 1.6 copy-start.20
  373.8 23.6 %all-to-all-start.2 = ((bf16[1,8,16,1600]{3,2,0,1:T(8,128)(2,1)}), bf16[1,8,16,1600]{3,2,0,1:T(8,128)(2,1)}, u32[]{:S(2)}, u32[]{:S(2)}) async-start(bf16[1,8,16,1600]{3,2,0,1:T(8,128)(2,1)} %bitcast.534), calls=%async_computation.2 | async-start | bytes 851968 | tf_op jit(solution)/shard_map/all_to_all | solution.py:137
  398.4 0.7 copy-start.30
  417.0 1.6 copy-start.8
  417.0 5.1 copy-start.41
  418.6 45.4 %copy-start.4 = (bf16[2,1,128,1600]{2,3,1,0:T(8,128)(2,1)S(1)}, bf16[2,1,128,1600]{2,3,1,0:T(8,128)(2,1)}, u32[]{:S(2)}) copy-start(bf16[2,1,128,1600]{2,3,1,0:T(8,128)(2,1)} %param.18) | copy-start | bytes 2457604
  420.1 45.0 %copy-start.22 = (bf16[1,128,1600]{1,2,0:T(8,128)(2,1)}, bf16[1,128,1600]{1,2,0:T(8,128)(2,1)S(1)}, u32[]{:S(2)}) copy-start(bf16[1,128,1600]{1,2,0:T(8,128)(2,1)S(1)} %fusion.133) | copy-start | bytes 1228804
  420.1 43.9 %collective-permute-start.2 = (bf16[1,128,1600]{1,2,0:T(8,128)(2,1)S(1)}, bf16[1,128,1600]{1,2,0:T(8,128)(2,1)S(1)}, u32[]{:S(2)}, u32[]{:S(2)}) collective-permute-start(bf16[1,128,1600]{1,2,0:T(8,128)(2,1)S(1)} %fusion.133), channel_id=1, source_target_pairs={{128,0},{256,128},{384,256},{129,1},{257,129},{385,257},{130,2},{2... | collective-permute-start | bytes 1228808 | tf_op jit(solution)/shard_map/ppermute | solution.py:20
  422.1 43.0 %copy-start.36 = (bf16[3,1,16,1600]{3,2,0,1:T(8,128)(2,1)}, bf16[3,1,16,1600]{3,2,0,1:T(8,128)(2,1)S(1)}, u32[]{:S(2)}) copy-start(bf16[3,1,16,1600]{3,2,0,1:T(8,128)(2,1)S(1)} %constant_dynamic-update-slice_fusion.14) | copy-start | bytes 460804
  492.2 1.6 copy-start.21
  501.3 21.3 %all-to-all-start.3 = ((bf16[1,8,16,1600]{3,2,0,1:T(8,128)(2,1)}), bf16[1,8,16,1600]{3,2,0,1:T(8,128)(2,1)}, u32[]{:S(2)}, u32[]{:S(2)}) async-start(bf16[1,8,16,1600]{3,2,0,1:T(8,128)(2,1)} %bitcast.536), calls=%async_computation.3 | async-start | bytes 851968 | tf_op jit(solution)/shard_map/all_to_all | solution.py:137
  523.7 0.6 copy-start.32
  542.3 1.6 copy-start.7
  546.1 44.2 %collective-permute-start.3 = (bf16[1,128,1600]{1,2,0:T(8,128)(2,1)}, bf16[1,128,1600]{1,2,0:T(8,128)(2,1)}, u32[]{:S(2)}, u32[]{:S(2)}) collective-permute-start(bf16[1,128,1600]{1,2,0:T(8,128)(2,1)} %fusion.127), channel_id=1, source_target_pairs={{128,0},{256,128},{384,256},{129,1},{257,129},{385,257},{130,2},{2... | collective-permute-start | bytes 1228808 | tf_op jit(solution)/shard_map/ppermute | solution.py:20
  594.7 7.8 copy-start.6
  594.7 7.8 copy-start.45
  596.7 103.9 %all-to-all-start.4 = ((bf16[1,8,16,1600]{3,2,0,1:T(8,128)(2,1)}), bf16[1,8,16,1600]{3,2,0,1:T(8,128)(2,1)}, u32[]{:S(2)}, u32[]{:S(2)}) async-start(bf16[1,8,16,1600]{3,2,0,1:T(8,128)(2,1)} %bitcast.151), calls=%async_computation.4 | async-start | bytes 851968 | tf_op jit(solution)/shard_map/all_to_all | solution.py:137
  602.5 3.8 copy-start.12
  684.4 11.5 copy-start.24
  685.4 10.5 collective-permute-start.4
  689.1 6.8 collective-permute-start.5
  693.2 3.4 copy-start.23
  693.2 3.4 copy-start.38
  693.2 3.4 copy-start.39
  697.1 4.7 copy-start.27
  697.1 4.7 copy-start.29
  697.1 4.7 copy-start.31
  697.1 4.7 copy-start.33
  700.6 18.5 %copy-start.10 = (f32[1,1,128,1600]{2,3,1,0:T(8,128)S(1)}, f32[1,1,128,1600]{2,3,1,0:T(8,128)}, u32[]{:S(2)}) copy-start(f32[1,1,128,1600]{2,3,1,0:T(8,128)} %copy.273) | copy-start | bytes 2457604
  703.2 16.3 %copy-start.17 = (bf16[1,128,1600]{1,2,0:T(8,128)(2,1)S(1)}, bf16[1,128,1600]{1,2,0:T(8,128)(2,1)}, u32[]{:S(2)}) copy-start(bf16[1,128,1600]{1,2,0:T(8,128)(2,1)} %get-tuple-element.408) | copy-start | bytes 1228804
  703.2 16.3 %copy-start.46 = (f32[16]{0:T(128)S(1)}, f32[16]{0:T(128)}, u32[]{:S(2)}) copy-start(f32[16]{0:T(128)} %dynamic-slice.8) | copy-start | bytes 196
  719.4 0.9 copy-start.37
Sparse Core Ops, SparseCore 0:
  11.6 67.1 all-gather.8
where the time goes:
time: 1410 us; the launch traced here: 1400 us
  blocking collectives  840 us (60%)
  waiting for transfers between devices  281 us (20%)
  local copies, waits for them, and re-layouts  143 us (10%)
  other arithmetic  47.2 us (3%)
  starting transfers between devices  37.3 us (3%)
  matrix products  31.9 us (2%)
  between operations  15.6 us (1%)
    psum x1, blocking collectives, local(): scale_grad, gain_grad = lax.psum((scale_part, gain_part), ('dp', 'tensor'))  668 us
    ppermute x4, waiting for transfers between devices, from_behind(): return lax.ppermute(block, axis, route)  213 us
    all_gather x5, blocking collectives, local(): lax.all_gather(own_d.astype(jnp.bfloat16), 'tensor', axis=1, tiled=True)  78.7 us
    unnamed x1, blocking collectives  76.2 us
    all_gather x1, waiting for transfers between devices, local(): lax.all_gather(master[0].astype(jnp.bfloat16), 'dp', axis=0, tiled=True)  50.7 us
    another operation x23, local copies, waits for them, and re-layouts  32.1 us
  transfers between devices with their start and end apart: 12, of which 8 were waited for; matrix products, arithmetic and copies ran while one was open for 11% of the time, Pallas kernels for 0%

commit v1 on v0

--- a/solution.py
+++ b/solution.py
@@ -173,7 +173,7 @@
         "mbsd,mbsc->dc", grad_kept, attended_flat, preferred_element_type=jnp.float32
     )
     scale_part = jnp.sum(w_out.astype(jnp.float32) * summed_out, axis=1)
-    scale_grad, gain_grad = lax.psum((scale_part, gain_part), ("dp", "tensor"))
+    scale_grad, gain_grad = lax.psum(lax.psum((scale_part, gain_part), "dp"), "tensor")
     bias_one = 1.0 - beta_one**adam_step
     bias_two = 1.0 - beta_two**adam_step
     first_new = beta_one * moment_one[0] + (1.0 - beta_one) * weight_grad

time: 1410 us -> 838 us (0.59)
  blocking collectives: 840 us -> 270 us
    psum x1 -> x2, blocking collectives: 668 us -> 97.7 us  [the longest x1 71.7 us: local(): lax.psum((scale_part, gain_part), 'dp')]
  transfers between devices with their start and end apart: 12 -> 12, of which waited for: 8 -> 8; matrix products, arithmetic and copies ran while one was open for 11% -> 18% of each run, Pallas kernels for 0% -> 0%
where the time goes in v1:
time: 838 us; the launch traced here: 826 us
  waiting for transfers between devices  281 us (34%)
  blocking collectives  270 us (32%)
  local copies, waits for them, and re-layouts  143 us (17%)
  other arithmetic  47.2 us (6%)
  starting transfers between devices  37.3 us (4%)
  matrix products  31.9 us (4%)
  between operations  15.6 us (2%)
    ppermute x4, waiting for transfers between devices, from_behind(): return lax.ppermute(block, axis, route)  213 us
    all_gather x5, blocking collectives, local(): lax.all_gather(own_d.astype(jnp.bfloat16), 'tensor', axis=1, tiled=True)  78.7 us
    unnamed x1, blocking collectives  76.2 us
    psum x1, blocking collectives, local(): lax.psum((scale_part, gain_part), 'dp')  71.7 us
    all_gather x1, waiting for transfers between devices, local(): lax.all_gather(master[0].astype(jnp.bfloat16), 'dp', axis=0, tiled=True)  50.7 us
    another operation x23, local copies, waits for them, and re-layouts  32.1 us
    psum x1, blocking collectives, local(): lax.psum(lax.psum((scale_part, gain_part), 'dp'), 'tensor')  25.9 us
    dynamic_update_slice x15, local copies, waits for them, and re-layouts, store_slot(): return lax.dynamic_update_index_in_dim(buffer, value, slot_index, 0)  21.4 us
  transfers between devices with their start and end apart: 12, of which 8 were waited for; matrix products, arithmetic and copies ran while one was open for 18% of the time, Pallas kernels for 0%

profile of v1, /device:TPU:128, one launch (start us, length us, event | category | flops | bytes accessed | tf_op | source)
XLA Modules:
  0.0 826.4 jit_solution(16303371203682361164)
XLA Ops:
  9.8 17.2 %all-gather = bf16[1,2,1,128,1600]{4,3,2,1,0:T(8,128)(2,1)S(1)} all-gather(bf16[1,2,1,16,1600]{4,3,2,1,0:T(8,128)(2,1)} %param.17), channel_id=2, replica_groups=mesh['pipe'=4,'dp'=16,'tensor'=8] {'tensor'}, dimensions={3}, use_global_device_ids=true | all-gather | bytes 921600 | tf_op jit(solution)/shard_map/all_gather | solution.py:54
  28.1 50.7 %all-gather.9.cloned.1.call-done = bf16[16,100,1024]{2,1,0:T(8,128)(2,1)} async-done(((bf16[1,100,1024]{2,1,0:T(8,128)(2,1)}), bf16[16,100,1024]{2,1,0:T(8,128)(2,1)}) %all-gather.9.cloned.1.call-update) | async-done | bytes 3276816 | tf_op jit(solution)/shard_map/all_gather | solution.py:51
  78.8 2.9 reshape.819
  81.7 3.4 fusion.113
  96.1 2.1 convolution_convert_fusion.20
  98.2 2.3 conditional.5
  100.5 2.0 copy.213
  102.5 4.8 all-to-all-start
  108.7 2.3 constant_dynamic-slice_fusion
  111.4 2.4 copy.217
  115.1 5.5 all-to-all-done
  122.4 15.6 %all-gather.1 = bf16[128,1600]{1,0:T(8,128)(2,1)} all-gather(bf16[16,1600]{1,0:T(8,128)(2,1)S(1)} %convert_element_type.421), channel_id=3, replica_groups=mesh['pipe'=4,'dp'=16,'tensor'=8] {'tensor'}, dimensions={0}, use_global_device_ids=true | all-gather | bytes 460800 | tf_op jit(solution)/shard_map/all_gather | solution.py:139
  138.0 1.9 copy.216
  141.5 2.2 fusion.145
  143.8 2.1 collective-permute-start
  147.2 39.6 %collective-permute-done = bf16[1,128,1600]{1,2,0:T(8,128)(2,1)} collective-permute-done((bf16[1,128,1600]{1,2,0:T(8,128)(2,1)}, bf16[1,128,1600]{1,2,0:T(8,128)(2,1)}, u32[]{:S(2)}, u32[]{:S(2)}) %collective-permute-start) | collective-permute-done | bytes 409632 | tf_op jit(solution)/shard_map/ppermute | solution.py:20
  186.9 1.9 bitcast_dynamic-update-slice_fusion.2
  189.9 2.7 conditional.6
  192.6 2.0 copy.227
  194.6 4.1 all-to-all-start.1
  198.7 2.4 copy.231
  201.1 10.9 %all-to-all-done.1 = bf16[1,8,16,1600]{3,2,0,1:T(8,128)(2,1)} async-done(((bf16[1,8,16,1600]{3,2,0,1:T(8,128)(2,1)}), bf16[1,8,16,1600]{3,2,0,1:T(8,128)(2,1)}, u32[]{:S(2)}, u32[]{:S(2)}) %all-to-all-start.1) | async-done | bytes 409632 | tf_op jit(solution)/shard_map/all_to_all | solution.py:137
  213.7 15.6 %all-gather.2 = bf16[128,1600]{1,0:T(8,128)(2,1)} all-gather(bf16[16,1600]{1,0:T(8,128)(2,1)S(1)} %convert_element_type.429), channel_id=4, replica_groups=mesh['pipe'=4,'dp'=16,'tensor'=8] {'tensor'}, dimensions={0}, use_global_device_ids=true | all-gather | bytes 460800 | tf_op jit(solution)/shard_map/all_gather | solution.py:139
  229.2 2.0 copy.230
  232.9 2.2 fusion.139
  235.1 2.2 collective-permute-start.1
  237.3 98.2 %collective-permute-done.1 = bf16[1,128,1600]{1,2,0:T(8,128)(2,1)} collective-permute-done((bf16[1,128,1600]{1,2,0:T(8,128)(2,1)}, bf16[1,128,1600]{1,2,0:T(8,128)(2,1)}, u32[]{:S(2)}, u32[]{:S(2)}) %collective-permute-start.1) | collective-permute-done | bytes 409632 | tf_op jit(solution)/shard_map/ppermute | solution.py:20
  335.5 2.1 bitcast_dynamic-update-slice_fusion.1
  337.7 34.1 %conditional.7 = (bf16[1,128,1600]{1,2,0:T(8,128)(2,1)}, bf16[1,1,128,768]{3,2,0,1:T(8,128)(2,1)}, bf16[1,1,128,1600]{2,3,0,1:T(8,128)(2,1)}) conditional(s32[]{:T(128)} %convert_element_type.434, () %tuple.72, (s32[]{:T(128)}, bf16[2,1,128,2,128]{4,2,3,0,1:T(8,128)(2,1)}, f32[2,1,2,128,128]{3,4,2,0,1:T(8,128)S(1)}, f32[1,1600]{1,0:T(1,128)S(1)}, ...), branch_computations={%region_11.12_spmd, %region_12.13_spmd} | conditional | flops 454803200 | bytes 11565162 | solution.py:133
  337.7 2.0 copy.236
  369.8 2.0 copy.364
  371.8 2.0 copy.241
  373.8 4.1 all-to-all-start.2
  377.9 2.3 copy.245
  380.3 2.3 copy.259
  382.6 2.4 copy.273
  399.1 16.0 %all-gather.3 = bf16[128,1600]{1,0:T(8,128)(2,1)} all-gather(bf16[16,1600]{1,0:T(8,128)(2,1)S(1)} %convert_element_type.437), channel_id=5, replica_groups=mesh['pipe'=4,'dp'=16,'tensor'=8] {'tensor'}, dimensions={0}, use_global_device_ids=true | all-gather | bytes 460800 | tf_op jit(solution)/shard_map/all_gather | solution.py:139
  415.0 1.9 copy.244
  425.6 38.5 %collective-permute-done.2 = bf16[1,128,1600]{1,2,0:T(8,128)(2,1)S(1)} collective-permute-done((bf16[1,128,1600]{1,2,0:T(8,128)(2,1)S(1)}, bf16[1,128,1600]{1,2,0:T(8,128)(2,1)S(1)}, u32[]{:S(2)}, u32[]{:S(2)}) %collective-permute-start.2) | collective-permute-done | bytes 409632 | tf_op jit(solution)/shard_map/ppermute | solution.py:20
  465.1 34.2 %conditional.8 = (bf16[1,128,1600]{1,2,0:T(8,128)(2,1)}, bf16[1,1,128,768]{3,2,0,1:T(8,128)(2,1)}, bf16[1,1,128,1600]{2,3,0,1:T(8,128)(2,1)}) conditional(s32[]{:T(128)} %convert_element_type.442, () %tuple.74, (s32[]{:T(128)}, bf16[2,1,128,2,128]{4,2,3,0,1:T(8,128)(2,1)}, f32[2,1,2,128,128]{3,4,2,0,1:T(8,128)S(1)}, f32[1,1600]{1,0:T(1,128)S(1)}, ...), branch_computations={%region_15.16_spmd, %region_16.17_spmd} | conditional | flops 454803200 | bytes 11565162 | solution.py:133
  465.2 2.0 copy.250
  467.8 1.9 convolution_convert_fusion.12
  497.4 1.9 copy.368
  499.3 2.0 copy.255
  501.3 4.1 all-to-all-start.3
  505.4 1.9 dynamic-slice_bitcast_fusion.2
  524.3 16.0 %all-gather.4 = bf16[128,1600]{1,0:T(8,128)(2,1)} all-gather(bf16[16,1600]{1,0:T(8,128)(2,1)S(1)} %convert_element_type.445), channel_id=6, replica_groups=mesh['pipe'=4,'dp'=16,'tensor'=8] {'tensor'}, dimensions={0}, use_global_device_ids=true | all-gather | bytes 460800 | tf_op jit(solution)/shard_map/all_gather | solution.py:139
  540.3 1.9 copy.258
  543.9 2.2 fusion.127
  546.1 2.1 collective-permute-start.3
  548.2 1.9 dynamic-slice_bitcast_fusion
  553.3 36.9 %collective-permute-done.3 = bf16[1,128,1600]{1,2,0:T(8,128)(2,1)} collective-permute-done((bf16[1,128,1600]{1,2,0:T(8,128)(2,1)}, bf16[1,128,1600]{1,2,0:T(8,128)(2,1)}, u32[]{:S(2)}, u32[]{:S(2)}) %collective-permute-start.3) | collective-permute-done | bytes 409632 | tf_op jit(solution)/shard_map/ppermute | solution.py:20
  590.2 2.2 bitcast_dynamic-update-slice_fusion.3
  592.4 2.3 conditional.9
  594.7 2.0 copy.269
  596.7 4.1 all-to-all-start.4
  602.5 1.9 bitcast_convert_fusion
  608.2 76.2 %fusion = bf16[112,1024]{1,0:T(8,128)(2,1)} fusion(bf16[1600,1024]{1,0:T(8,128)(2,1)S(1)} %pad_maximum_fusion.5), kind=kCustom, calls=%all-reduce-scatter | all-reduce-scatter fusion | flops 1835009 | bytes 3508224
  685.4 3.7 collective-permute-start.4
  689.1 4.1 collective-permute-start.5
  693.2 2.0 fusion.112
  703.2 15.6 %all-gather.5 = bf16[128,1600]{1,0:T(8,128)(2,1)S(1)} all-gather(bf16[16,1600]{1,0:T(8,128)(2,1)S(1)} %get-tuple-element.432), channel_id=7, replica_groups=mesh['pipe'=4,'dp'=16,'tensor'=8] {'tensor'}, dimensions={0}, use_global_device_ids=true | all-gather | bytes 460800 | tf_op jit(solution)/shard_map/all_gather | solution.py:139
  721.0 71.7 %all-reduce.2 = (f32[1600]{0:T(1024)S(1)}, f32[1600]{0:T(1024)S(1)}) all-reduce(f32[1600]{0:T(1024)S(1)} %select_add_fusion, f32[1600]{0:T(1024)S(1)} %fusion.112), channel_id=1, replica_groups=mesh['pipe'=4,'dp'=16,'tensor'=8] {'dp'}, use_global_device_ids=true, to_apply=%region_32.33 | all-reduce | flops 3200 | bytes 25600 | tf_op jit(solution)/shard_map/psum | solution.py:176
  792.8 25.9 %all-reduce.3 = (f32[1,1600]{1,0:T(1,128)S(1)}, f32[1,1600]{1,0:T(1,128)S(1)}) all-reduce(f32[1,1600]{1,0:T(1,128)S(1)} %stack.10, f32[1,1600]{1,0:T(1,128)S(1)} %stack.9), channel_id=1, replica_groups=mesh['pipe'=4,'dp'=16,'tensor'=8] {'tensor'}, use_global_device_ids=true, to_apply=%region_33.34 | all-reduce | flops 3200 | bytes 25600 | tf_op jit(solution)/shard_map/psum | solution.py:176
  (216 shorter events, 153.9 us)
Async XLA Ops:
  7.2 20.1 %copy-start.2 = (bf16[2,1,128,1600]{2,3,1,0:T(8,128)(2,1)S(1)}, bf16[2,1,128,1600]{2,3,1,0:T(8,128)(2,1)}, u32[]{:S(2)}) copy-start(bf16[2,1,128,1600]{2,3,1,0:T(8,128)(2,1)} %param.18) | copy-start | bytes 2457604
  7.2 71.6 %all-gather.9.cloned.1.call-start = ((), (), s32[]{:S(2)}) async-start(), calls=%async_computation.5 | async-start | bytes 3620864 | tf_op jit(solution)/shard_map/all_gather | solution.py:51
  27.0 1.1 copy-start.5
  27.3 54.4 %copy-start.44 = (f32[2,128]{1,0:T(2,128)}, f32[2,128]{1,0:T(2,128)S(1)}, u32[]{:S(2)}) copy-start(f32[2,128]{1,0:T(2,128)S(1)} %add_rsqrt_fusion) | copy-start | bytes 3076
  81.7 3.5 copy-start.1
  88.3 0.8 copy-start.35
  88.3 5.4 copy-start.34
  93.7 4.5 copy-start.42
  102.5 18.2 %all-to-all-start = ((bf16[1,8,16,1600]{3,2,0,1:T(8,128)(2,1)}), bf16[1,8,16,1600]{3,2,0,1:T(8,128)(2,1)}, u32[]{:S(2)}, u32[]{:S(2)}) async-start(bf16[1,8,16,1600]{3,2,0,1:T(8,128)(2,1)} %bitcast.535), calls=%async_computation | async-start | bytes 851968 | tf_op jit(solution)/shard_map/all_to_all | solution.py:137
  108.6 2.7 copy-start
  121.7 0.6 copy-start.26
  139.9 1.6 copy-start.11
  143.8 43.1 %collective-permute-start = (bf16[1,128,1600]{1,2,0:T(8,128)(2,1)}, bf16[1,128,1600]{1,2,0:T(8,128)(2,1)}, u32[]{:S(2)}, u32[]{:S(2)}) collective-permute-start(bf16[1,128,1600]{1,2,0:T(8,128)(2,1)} %fusion.145), channel_id=1, source_target_pairs={{128,0},{256,128},{384,256},{129,1},{257,129},{385,257},{130,2},{2... | collective-permute-start | bytes 1228808 | tf_op jit(solution)/shard_map/ppermute | solution.py:20
  145.9 41.0 %copy-start.3 = (bf16[2,1,128,1600]{2,3,1,0:T(8,128)(2,1)S(1)}, bf16[2,1,128,1600]{2,3,1,0:T(8,128)(2,1)}, u32[]{:S(2)}) copy-start(bf16[2,1,128,1600]{2,3,1,0:T(8,128)(2,1)} %param.18) | copy-start | bytes 2457604
  188.8 1.1 copy-start.25
  194.6 17.4 %all-to-all-start.1 = ((bf16[1,8,16,1600]{3,2,0,1:T(8,128)(2,1)}), bf16[1,8,16,1600]{3,2,0,1:T(8,128)(2,1)}, u32[]{:S(2)}, u32[]{:S(2)}) async-start(bf16[1,8,16,1600]{3,2,0,1:T(8,128)(2,1)} %bitcast.537), calls=%async_computation.1 | async-start | bytes 851968 | tf_op jit(solution)/shard_map/all_to_all | solution.py:137
  213.0 0.6 copy-start.28
  231.2 1.6 copy-start.9
  235.1 100.4 %collective-permute-start.1 = (bf16[1,128,1600]{1,2,0:T(8,128)(2,1)}, bf16[1,128,1600]{1,2,0:T(8,128)(2,1)}, u32[]{:S(2)}, u32[]{:S(2)}) collective-permute-start(bf16[1,128,1600]{1,2,0:T(8,128)(2,1)} %fusion.139), channel_id=1, source_target_pairs={{128,0},{256,128},{384,256},{129,1},{257,129},{385,257},{130,2},{2... | collective-permute-start | bytes 1228808 | tf_op jit(solution)/shard_map/ppermute | solution.py:20
  364.7 1.6 copy-start.20
  373.8 23.6 %all-to-all-start.2 = ((bf16[1,8,16,1600]{3,2,0,1:T(8,128)(2,1)}), bf16[1,8,16,1600]{3,2,0,1:T(8,128)(2,1)}, u32[]{:S(2)}, u32[]{:S(2)}) async-start(bf16[1,8,16,1600]{3,2,0,1:T(8,128)(2,1)} %bitcast.534), calls=%async_computation.2 | async-start | bytes 851968 | tf_op jit(solution)/shard_map/all_to_all | solution.py:137
  398.4 0.7 copy-start.30
  417.0 1.6 copy-start.8
  417.0 5.1 copy-start.41
  418.6 45.4 %copy-start.4 = (bf16[2,1,128,1600]{2,3,1,0:T(8,128)(2,1)S(1)}, bf16[2,1,128,1600]{2,3,1,0:T(8,128)(2,1)}, u32[]{:S(2)}) copy-start(bf16[2,1,128,1600]{2,3,1,0:T(8,128)(2,1)} %param.18) | copy-start | bytes 2457604
  420.1 45.0 %copy-start.22 = (bf16[1,128,1600]{1,2,0:T(8,128)(2,1)}, bf16[1,128,1600]{1,2,0:T(8,128)(2,1)S(1)}, u32[]{:S(2)}) copy-start(bf16[1,128,1600]{1,2,0:T(8,128)(2,1)S(1)} %fusion.133) | copy-start | bytes 1228804
  420.1 43.9 %collective-permute-start.2 = (bf16[1,128,1600]{1,2,0:T(8,128)(2,1)S(1)}, bf16[1,128,1600]{1,2,0:T(8,128)(2,1)S(1)}, u32[]{:S(2)}, u32[]{:S(2)}) collective-permute-start(bf16[1,128,1600]{1,2,0:T(8,128)(2,1)S(1)} %fusion.133), channel_id=1, source_target_pairs={{128,0},{256,128},{384,256},{129,1},{257,129},{385,257},{130,2},{2... | collective-permute-start | bytes 1228808 | tf_op jit(solution)/shard_map/ppermute | solution.py:20
  422.1 43.0 %copy-start.36 = (bf16[3,1,16,1600]{3,2,0,1:T(8,128)(2,1)}, bf16[3,1,16,1600]{3,2,0,1:T(8,128)(2,1)S(1)}, u32[]{:S(2)}) copy-start(bf16[3,1,16,1600]{3,2,0,1:T(8,128)(2,1)S(1)} %constant_dynamic-update-slice_fusion.14) | copy-start | bytes 460804
  492.2 1.6 copy-start.21
  501.3 21.3 %all-to-all-start.3 = ((bf16[1,8,16,1600]{3,2,0,1:T(8,128)(2,1)}), bf16[1,8,16,1600]{3,2,0,1:T(8,128)(2,1)}, u32[]{:S(2)}, u32[]{:S(2)}) async-start(bf16[1,8,16,1600]{3,2,0,1:T(8,128)(2,1)} %bitcast.536), calls=%async_computation.3 | async-start | bytes 851968 | tf_op jit(solution)/shard_map/all_to_all | solution.py:137
  523.7 0.6 copy-start.32
  542.3 1.6 copy-start.7
  546.1 44.2 %collective-permute-start.3 = (bf16[1,128,1600]{1,2,0:T(8,128)(2,1)}, bf16[1,128,1600]{1,2,0:T(8,128)(2,1)}, u32[]{:S(2)}, u32[]{:S(2)}) collective-permute-start(bf16[1,128,1600]{1,2,0:T(8,128)(2,1)} %fusion.127), channel_id=1, source_target_pairs={{128,0},{256,128},{384,256},{129,1},{257,129},{385,257},{130,2},{2... | collective-permute-start | bytes 1228808 | tf_op jit(solution)/shard_map/ppermute | solution.py:20
  594.7 7.8 copy-start.6
  594.7 7.8 copy-start.45
  596.7 103.9 %all-to-all-start.4 = ((bf16[1,8,16,1600]{3,2,0,1:T(8,128)(2,1)}), bf16[1,8,16,1600]{3,2,0,1:T(8,128)(2,1)}, u32[]{:S(2)}, u32[]{:S(2)}) async-start(bf16[1,8,16,1600]{3,2,0,1:T(8,128)(2,1)} %bitcast.151), calls=%async_computation.4 | async-start | bytes 851968 | tf_op jit(solution)/shard_map/all_to_all | solution.py:137
  602.5 3.8 copy-start.12
  684.4 11.5 %copy-start.24 = (bf16[112,1024]{1,0:T(8,128)(2,1)S(1)}, bf16[112,1024]{1,0:T(8,128)(2,1)}, u32[]{:S(2)}) copy-start(bf16[112,1024]{1,0:T(8,128)(2,1)} %fusion) | copy-start | bytes 688132
  685.4 10.5 %collective-permute-start.4 = (bf16[112,1024]{1,0:T(8,128)(2,1)}, bf16[112,1024]{1,0:T(8,128)(2,1)S(1)}, u32[]{:S(2)}, u32[]{:S(2)}) collective-permute-start(bf16[112,1024]{1,0:T(8,128)(2,1)} %fusion), channel_id=1, source_target_pairs={{0,8},{8,16},{16,24},{24,32},{32,40},{40,48},{48,56},{56,64},{64,7... | collective-permute-start | bytes 688136
  689.1 6.8 collective-permute-start.5
  693.2 3.4 copy-start.23
  693.2 3.4 copy-start.38
  693.2 3.4 copy-start.39
  697.1 4.7 copy-start.27
  697.1 4.7 copy-start.29
  697.1 4.7 copy-start.31
  697.1 4.7 copy-start.33
  700.6 18.5 %copy-start.10 = (f32[1,1,128,1600]{2,3,1,0:T(8,128)S(1)}, f32[1,1,128,1600]{2,3,1,0:T(8,128)}, u32[]{:S(2)}) copy-start(f32[1,1,128,1600]{2,3,1,0:T(8,128)} %copy.273) | copy-start | bytes 2457604
  703.2 16.3 %copy-start.17 = (bf16[1,128,1600]{1,2,0:T(8,128)(2,1)S(1)}, bf16[1,128,1600]{1,2,0:T(8,128)(2,1)}, u32[]{:S(2)}) copy-start(bf16[1,128,1600]{1,2,0:T(8,128)(2,1)} %get-tuple-element.410) | copy-start | bytes 1228804
  703.2 16.3 %copy-start.46 = (f32[16]{0:T(128)S(1)}, f32[16]{0:T(128)}, u32[]{:S(2)}) copy-start(f32[16]{0:T(128)} %dynamic-slice.8) | copy-start | bytes 196
  719.4 0.9 copy-start.37
Sparse Core Ops, SparseCore 0:
  11.6 67.1 all-gather.8
